TPU v7x, 256 devices: a whole 4x4x8 slice. The times are simulated.
256 devices in a mesh: queue: 32 (over z_lo, x, core), head: 8 (over y, z_hi).
Axes of the slice: x: 4, y: 4, z: 8 (z_hi: 2, z_lo: 4; z = z_hi * 4 + z_lo), core: 2. Of those that a mesh axis runs over, the one named last changes fastest.
Arguments:
- latents: bfloat16 [128, 192, 3072], P('queue', 'head'), may hold values from -1.5 to 1.5
- queries: bfloat16 [128, 192, 3072], P('queue', 'head'), may hold values from -100 to 100
- key_proj: bfloat16 [128, 192, 3072], P('queue', 'head'), may hold values from -6.75 to 6.75
- values: bfloat16 [128, 192, 3072], P('queue', 'head'), may hold values from -48 to 48
- slot_steps: int32 [128], P('queue'), may hold values from 0 to 127
- noise_frame: bfloat16 [192, 3072], P('head'), may hold values from -6 to 6
Outputs:
- queue_next: bfloat16 [128, 192, 3072], P('queue', 'head')
- denoised: bfloat16 [128, 192, 3072], P('queue', 'head')
- finished: bfloat16 [192, 3072], P('head', 'queue')
All inputs are finite; a program needn't handle non-finite values.
Results may differ from a plain program's by a relative error of at most 0.007.
Values may be sent and summed in bfloat16 or wider, within the bound.
A program may use at most 128 MiB of HBM per device.

v0:
```python
import math

import jax
import jax.numpy as jnp
from jax import lax
from jax.sharding import PartitionSpec as P

HEADS = 24
HEAD_DIM = 128


shift_factor = 3.0


def padded(cells, sides, width):
    for axis, dim in sides:
        count = lax.axis_size(axis)
        ends = count - 1
        head = lax.slice_in_dim(cells, 0, width, axis=dim)
        tail = lax.slice_in_dim(cells, cells.shape[dim] - width, cells.shape[dim], axis=dim)
        cells = jnp.concatenate(
            [
                lax.ppermute(tail, axis, [(i, (i + 1) % count) for i in range(ends)]),
                cells,
                lax.ppermute(head, axis, [((i + 1) % count, i) for i in range(ends)]),
            ],
            axis=dim,
        )
    return cells


def shifted(shard, axis, by):
    peers = lax.axis_size(axis)
    pairs = [(i, i + by) for i in range(peers) if 0 <= i + by < peers]
    return lax.ppermute(shard, axis, pairs)


def from_root(shard, axis, root):
    mine = lax.axis_index(axis) == root
    return lax.psum(jnp.where(mine, shard, jnp.zeros_like(shard)), axis)


def noise_level(step_index, total):
    fraction = 1.0 - step_index.astype(jnp.float32) / total
    return shift_factor * fraction / (1.0 + (shift_factor - 1.0) * fraction)


def shards(latents, queries, key_proj, values, slot_steps, noise_frame):
    frames = latents.shape[0]
    queue_index = lax.axis_index("queue")
    queue_count = lax.axis_size("queue")
    block_id = jnp.arange(3 * frames, dtype=jnp.int32) // frames
    allowed = ((block_id != 0) | (queue_index > 0)) & (
        (block_id != 2) | (queue_index < queue_count - 1)
    )
    scale = 1.0 / math.sqrt(HEAD_DIM)
    stacked = jnp.stack([key_proj, values])
    extended = padded(stacked, (("queue", 1),), frames)
    local_rows = queries.shape[0] * queries.shape[1]
    query_split = queries.reshape(local_rows, HEADS, HEAD_DIM).transpose(1, 0, 2)
    start_state = (
        jnp.full((HEADS, local_rows), -jnp.inf, jnp.float32),
        jnp.zeros((HEADS, local_rows), jnp.float32),
        jnp.zeros((HEADS, local_rows, HEAD_DIM), jnp.float32),
    )
    piece = lax.all_gather(extended, "head", axis=2, tiled=True)
    piece_rows = piece.shape[2]
    key_piece = piece[0].reshape(3 * frames * piece_rows, HEADS, HEAD_DIM).transpose(1, 0, 2)
    value_piece = piece[1].reshape(3 * frames * piece_rows, HEADS, HEAD_DIM).transpose(1, 0, 2)
    keep_rows = jnp.repeat(allowed, piece_rows)

    def one_head(operands):
        query_head, key_head, value_head, running_top, running_total, running_sum = operands
        scores = (
            jnp.einsum("qd,kd->qk", query_head, key_head, preferred_element_type=jnp.float32)
            * scale
        )
        scores = jnp.where(keep_rows[None, :], scores, -jnp.inf)
        new_top = jnp.maximum(running_top, jnp.max(scores, axis=1))
        correction = jnp.exp(running_top - new_top)
        weights = jnp.where(keep_rows[None, :], jnp.exp(scores - new_top[:, None]), 0.0)
        new_total = running_total * correction + jnp.sum(weights, axis=1)
        product = jnp.dot(
            weights.astype(jnp.bfloat16), value_head, preferred_element_type=jnp.float32
        )
        new_sum = running_sum * correction[:, None] + product
        return (new_top, new_total, new_sum)

    final_top, final_total, final_sum = lax.map(
        one_head,
        (query_split, key_piece, value_piece, start_state[0], start_state[1], start_state[2]),
    )
    mixed = final_sum / final_total[:, :, None]
    attended = mixed.transpose(1, 0, 2).reshape(queries.shape).astype(jnp.bfloat16)
    velocity = lax.optimization_barrier(attended)
    steps_total = frames * queue_count
    level = noise_level(slot_steps, steps_total)[:, None, None]
    level_next = noise_level(slot_steps + 1, steps_total)[:, None, None]
    latent_wide = latents.astype(jnp.float32)
    velocity_wide = velocity.astype(jnp.float32)
    updated = (latent_wide + (level_next - level) * velocity_wide).astype(jnp.bfloat16)
    denoised = (latent_wide - level * velocity_wide).astype(jnp.bfloat16)
    leaving = updated[frames - 1]
    arriving = shifted(leaving, "queue", 1)
    arriving = jnp.where(queue_index == 0, noise_frame, arriving)
    queue_next = jnp.concatenate([arriving[None], updated[: frames - 1]], 0)
    whole_frame = from_root(leaving, "queue", queue_count - 1)
    column_count = whole_frame.shape[1] // queue_count
    finished = lax.dynamic_slice_in_dim(whole_frame, queue_index * column_count, column_count, 1)
    return (queue_next, denoised, finished)


def solution(mesh):
    return jax.shard_map(
        shards,
        mesh=mesh,
        in_specs=(
            P("queue", "head", None),
            P("queue", "head", None),
            P("queue", "head", None),
            P("queue", "head", None),
            P("queue"),
            P("head", None),
        ),
        out_specs=(P("queue", "head", None), P("queue", "head", None), P("head", "queue")),
        check_vma=False,
    )
```

profile of v0, /device:TPU:32, one launch (start us, length us, event | category | flops | bytes accessed | tf_op | source)
XLA Modules:
  0.0 907.2 jit_solution(9962514914455139318)
XLA Ops:
  7.2 1.4 pad_maximum_fusion.1
  8.7 1.9 collective-permute-start
  10.6 5.8 collective-permute-start.1
  16.4 11.9 %collective-permute-done = bf16[2,4,24,3072]{3,2,1,0:T(8,128)(2,1)S(1)} collective-permute-done((bf16[2,4,24,3072]{3,2,1,0:T(8,128)(2,1)S(1)}, bf16[2,4,24,3072]{3,2,1,0:T(8,128)(2,1)S(1)}, u32[]{:S(2)}, u32[]{:S(2)}) %collective-permute-start) | collective-permute-done | bytes 1179680 | tf_op jit(solution)/shard_map/ppermute | solution.py:23
  28.3 1.8 collective-permute-done.1
  30.1 2.0 pad_maximum_fusion
  33.8 490.3 %all-gather.2.cloned.1.call-done = bf16[2,12,192,3072]{3,2,1,0:T(8,128)(2,1)} async-done(((bf16[2,12,24,3072]{3,2,1,0:T(8,128)(2,1)}), bf16[2,12,192,3072]{3,2,1,0:T(8,128)(2,1)}) %all-gather.2.cloned.1.call-update) | async-done | bytes 28311568 | tf_op jit(solution)/shard_map/all_gather | solution.py:66
  524.1 11.5 %fusion.24 = (bf16[1,12,192,3072]{3,2,1,0:T(8,128)(2,1)S(1)}, bf16[1,12,192,3072]{3,2,1,0:T(8,128)(2,1)S(1)}) fusion(bf16[2,12,192,3072]{3,2,1,0:T(8,128)(2,1)} %all-gather.2.cloned.1.call-done), kind=kLoop, calls=%fused_computation.46 | loop fusion | bytes 56623104 | tf_op jit(solution)/shard_map/slice | solution.py:69
  535.6 6.9 copy.15
  542.5 14.0 %copy.11 = bf16[24,2304,128]{2,1,0:T(8,128)(2,1)} copy(bf16[24,2304,128]{2,0,1:T(8,128)(2,1)} %bitcast.56) | data formatting | bytes 28311552
  556.6 3.5 copy.16
  560.0 6.5 copy.12
  566.5 83.2 %while.13 = (s32[]{:T(128)}, f32[24,96]{1,0:T(8,128)S(1)}, f32[24,96,128]{2,1,0:T(8,128)S(1)}, bf16[24,96,128]{2,1,0:T(8,128)(2,1)S(1)}, bf16[24,2304,128]{2,1,0...) while((s32[]{:T(128)}, f32[24,96]{1,0:T(8,128)S(1)}, ...), condition=%wide.region_3.4_spmd.clone, body=%wide.region_0.3_spmd.clone.sunk | while | flops 115249248 | bytes 3929581 | solution.py:89
  566.7 1.5 fusion.32
  570.2 1.5 fusion.32
  573.6 1.5 fusion.32
  577.1 1.5 fusion.32
  578.9 1.4 fusion.34
  580.6 1.5 fusion.32
  584.0 1.5 fusion.32
  585.9 1.4 fusion.34
  587.5 1.5 fusion.32
  591.0 1.5 fusion.32
  592.8 1.4 fusion.34
  594.4 1.5 fusion.32
  597.9 1.5 fusion.32
  599.7 1.4 fusion.34
  601.3 1.5 fusion.32
  604.8 1.5 fusion.32
  606.6 1.4 fusion.34
  608.3 1.5 fusion.32
  611.7 1.5 fusion.32
  613.6 1.4 fusion.34
  615.2 1.5 fusion.32
  618.7 1.5 fusion.32
  620.5 1.4 fusion.34
  622.1 1.5 fusion.32
  625.6 1.5 fusion.32
  629.1 1.5 fusion.32
  632.5 1.5 fusion.32
  634.4 1.4 fusion.34
  636.0 1.5 fusion.32
  639.5 1.5 fusion.32
  642.9 1.5 fusion.32
  646.4 1.5 fusion.32
  652.3 2.1 collective-permute-start.2
  655.1 6.4 collective-permute-done.2
  662.4 236.6 %all-reduce.2.cloned.1.call-done = bf16[24,3072]{1,0:T(8,128)(2,1)} async-done(((bf16[24,3072]{1,0:T(8,128)(2,1)}), bf16[24,3072]{1,0:T(8,128)(2,1)}) %all-reduce.2.cloned.1.call-update) | async-done | bytes 147472 | tf_op jit(solution)/shard_map/psum | solution.py:40
  (168 shorter events, 42.6 us)
Async XLA Ops:
  7.2 517.0 %all-gather.2.cloned.1.call-start = ((), (), s32[]{:S(2)}) async-start(), calls=%async_computation | async-start | bytes 31850496 | tf_op jit(solution)/shard_map/all_gather | solution.py:66
  7.2 22.9 %copy-start = (bf16[4,24,3072]{2,1,0:T(8,128)(2,1)S(1)}, bf16[4,24,3072]{2,1,0:T(8,128)(2,1)}, u32[]{:S(2)}) copy-start(bf16[4,24,3072]{2,1,0:T(8,128)(2,1)} %param.11) | copy-start | bytes 1769476
  7.2 22.9 %copy-start.1 = (bf16[4,24,3072]{2,1,0:T(8,128)(2,1)S(1)}, bf16[4,24,3072]{2,1,0:T(8,128)(2,1)}, u32[]{:S(2)}) copy-start(bf16[4,24,3072]{2,1,0:T(8,128)(2,1)} %param.10) | copy-start | bytes 1769476
  8.7 19.6 %collective-permute-start = (bf16[2,4,24,3072]{3,2,1,0:T(8,128)(2,1)S(1)}, bf16[2,4,24,3072]{3,2,1,0:T(8,128)(2,1)S(1)}, u32[]{:S(2)}, u32[]{:S(2)}) collective-permute-start(bf16[2,4,24,3072]{3,2,1,0:T(8,128)(2,1)S(1)} %pad_maximum_fusion.1), channel_id=1, source_target_pairs={{0,8},{8,16},{16,24},{24,32},{32,40},{40,48},{48,56},{56,64},{64,7... | collective-permute-start | bytes 3538952 | tf_op jit(solution)/shard_map/ppermute | solution.py:23
  10.6 19.5 %collective-permute-start.1 = (bf16[2,4,24,3072]{3,2,1,0:T(8,128)(2,1)S(1)}, bf16[2,4,24,3072]{3,2,1,0:T(8,128)(2,1)S(1)}, u32[]{:S(2)}, u32[]{:S(2)}) collective-permute-start(bf16[2,4,24,3072]{3,2,1,0:T(8,128)(2,1)S(1)} %pad_maximum_fusion.1), channel_id=1, source_target_pairs={{8,0},{16,8},{24,16},{32,24},{40,32},{48,40},{56,48},{64,56},{72,6... | collective-permute-start | bytes 3538952 | tf_op jit(solution)/shard_map/ppermute | solution.py:25
  32.1 1.1 copy-start.2
  32.1 866.8 %all-reduce.2.cloned.1.call-start = ((), (), s32[]{:S(2)}) async-start(), calls=%async_computation.1 | async-start | bytes 294912 | tf_op jit(solution)/shard_map/psum | solution.py:40
  33.2 0.7 copy-start.5
  650.1 1.1 copy-start.3
  652.3 9.2 %copy-start.4 = (bf16[24,3072]{1,0:T(8,128)(2,1)S(1)}, bf16[24,3072]{1,0:T(8,128)(2,1)}, u32[]{:S(2)}) copy-start(bf16[24,3072]{1,0:T(8,128)(2,1)} %param.13) | copy-start | bytes 442372
  652.3 9.2 %collective-permute-start.2 = (bf16[24,3072]{1,0:T(8,128)(2,1)S(1)}, bf16[24,3072]{1,0:T(8,128)(2,1)S(1)}, u32[]{:S(2)}, u32[]{:S(2)}) collective-permute-start(bf16[24,3072]{1,0:T(8,128)(2,1)S(1)} %slice_bitcast_fusion), channel_id=1, source_target_pairs={{0,8},{8,16},{16,24},{24,32},{32,40},{40,48},{48,56},{56,64},{64,7... | collective-permute-start | bytes 442376 | tf_op jit(solution)/shard_map/ppermute | solution.py:35
Sparse Core Ops, SparseCore 0:
  32.3 491.8 all-gather.1
  655.3 243.6 all-reduce.1
where the time goes:
time: 921 us; the launch traced here: 907 us
  waiting for transfers between devices  747 us (81%)
  matrix products  69.7 us (8%)
  local copies, waits for them, and re-layouts  51.3 us (6%)
  other arithmetic  14.6 us (2%)
  between operations  14.2 us (2%)
  starting transfers between devices  9.8 us (1%)
    all_gather x1, waiting for transfers between devices, shards(): piece = lax.all_gather(extended, 'head', axis=2, tiled=True)  490 us
    psum x1, waiting for transfers between devices, from_root(): return lax.psum(jnp.where(mine, shard, jnp.zeros_like(shard)), axis)  237 us
    dot_general x24, matrix products, one_head(): jnp.einsum('qd,kd->qk', query_head, key_head, preferred_element_type=jnp....  35.9 us
    dot_general x24, matrix products, one_head(): jnp.dot(weights.astype(jnp.bfloat16), value_head, preferred_element_type=...  33.8 us
    unnamed x18, local copies, waits for them, and re-layouts  33.1 us
  transfers between devices with their start and end apart: 5, of which 5 were waited for; matrix products, arithmetic and copies ran while one was open for 0% of the time, Pallas kernels for 0%

commit v1 on v0

v1 whole, which is shorter than its diff:
```python
import functools
import math

import jax
import jax.numpy as jnp
from jax import lax
from jax.experimental import pallas as pl
from jax.experimental.pallas import tpu as pltpu
from jax.sharding import PartitionSpec as P

MESH = pl.DeviceIdType.MESH
HEADS = 24
HEAD_DIM = 128
D = HEADS * HEAD_DIM
FRAMES = 4
TOKENS = 24
ROWS = FRAMES * TOKENS
SHARES = 8
CLASSES = 3
WINDOW = ROWS * SHARES
CONTEXT = 3 * WINDOW
N_QUEUE = 32
STEPS = 128
HALF = N_QUEUE // 2
CHUNK = 256
PAD = 32
COLUMNS = D // N_QUEUE
SCALE = math.log2(math.e) / math.sqrt(HEAD_DIM)
shift_factor = 3.0


def noise_level(step_index):
    fraction = 1.0 - step_index / float(STEPS)
    return shift_factor * fraction / (1.0 + (shift_factor - 1.0) * fraction)


def kernel(
    q_hbm, k_hbm, v_hbm, lat_hbm, noise_ref, steps_ref,
    next_ref, den_ref, fin_ref,
    qbuf, kbuf, vbuf, obuf, vel, lat, leave, arrive, fin_stage, fin_land,
    send_q, send_k, send_v, recv_q, recv_k, recv_v,
    send_n, recv_kl, recv_kr, recv_vl, recv_vr,
    send_o, recv_o, send_l, recv_l, send_f, recv_f, lat_sem,
):
    q = lax.axis_index("queue")
    h = lax.axis_index("head")
    y, z_hi = h // 2, h % 2
    z_lo = q // 8
    far = (q + HALF) % N_QUEUE

    def flip(window):
        return (window // 16) % 2

    s_mine = (z_hi + flip(far)) % 2
    site_id = y * 2 + s_mine
    window = far

    def site_of(win, ident):
        return ((win + HALF) % N_QUEUE, (ident // 2) * 2 + (ident + flip(win)) % 2)

    has_left = window > 0
    has_right = window < N_QUEUE - 1
    left_site = site_of((window + N_QUEUE - 1) % N_QUEUE, site_id)
    right_site = site_of((window + 1) % N_QUEUE, site_id)

    lat_copy = pltpu.make_async_copy(lat_hbm, lat, lat_sem)
    lat_copy.start()

    barrier = pltpu.get_barrier_semaphore()

    def greet(device):
        pl.semaphore_signal(barrier, inc=1, device_id=device, device_id_type=MESH)

    @pl.loop(0, SHARES)
    def _(i):
        greet((far, i))

    @pl.when(has_left)
    def _():
        greet(left_site)

    @pl.when(has_right)
    def _():
        greet(right_site)

    @pl.when(q > 0)
    def _():
        greet((q - 1, h))

    @pl.when(q < N_QUEUE - 1)
    def _():
        greet((q + 1, h))
        greet((N_QUEUE - 1, h))

    @pl.when(q == N_QUEUE - 1)
    def _():
        @pl.loop(0, N_QUEUE - 1)
        def _(i):
            greet((i, h))

    edges = SHARES + has_left.astype(jnp.int32) + has_right.astype(jnp.int32)
    edges = edges + (q > 0).astype(jnp.int32) + 2 * (q < N_QUEUE - 1).astype(jnp.int32)
    edges = edges + (N_QUEUE - 1) * (q == N_QUEUE - 1).astype(jnp.int32)
    pl.semaphore_wait(barrier, edges)

    def scatter(src, dst, send, recv, j, row0):
        @pl.loop(0, SHARES)
        def _(i):
            column = pl.multiple_of((i * CLASSES + j) * HEAD_DIM, HEAD_DIM)
            row = pl.multiple_of(row0 + h * ROWS, 16)
            pltpu.make_async_remote_copy(
                src_ref=src.at[:, pl.ds(column, HEAD_DIM)],
                dst_ref=dst.at[j, pl.ds(row, ROWS), :],
                send_sem=send,
                recv_sem=recv.at[j],
                device_id=site_of(q, i),
                device_id_type=MESH,
            ).start()

    def scatter_class(j):
        scatter(k_hbm, kbuf, send_k, recv_k, j, WINDOW)
        scatter(v_hbm, vbuf, send_v, recv_v, j, WINDOW)
        scatter(q_hbm, qbuf, send_q, recv_q, j, 0)

    def await_recv(ref, sem):
        pltpu.make_async_copy(ref, ref, sem).wait()

    def own(buf, j):
        return buf.at[j, pl.ds(WINDOW, WINDOW), :]

    def pass_on(buf, j, side, recv, device, slot):
        return pltpu.make_async_remote_copy(
            src_ref=own(buf, j),
            dst_ref=buf.at[j, pl.ds(slot * WINDOW, WINDOW), :],
            send_sem=send_n.at[side, j],
            recv_sem=recv.at[j],
            device_id=device,
            device_id_type=MESH,
        )

    def forward(j):
        for n, (buf, recv, recv_left, recv_right) in enumerate(
            ((kbuf, recv_k, recv_kl, recv_kr), (vbuf, recv_v, recv_vl, recv_vr))
        ):
            await_recv(own(buf, j), recv.at[j])

            @pl.when(has_right)
            def _():
                pass_on(buf, j, 2 * n, recv_left, right_site, 0).start()

            @pl.when(has_left)
            def _():
                pass_on(buf, j, 2 * n + 1, recv_right, left_site, 2).start()

    left_flag = has_left.astype(jnp.float32)
    right_flag = has_right.astype(jnp.float32)

    def gather_context(j):
        @pl.when(has_left)
        def _():
            await_recv(kbuf.at[j, pl.ds(0, WINDOW), :], recv_kl.at[j])
            await_recv(vbuf.at[j, pl.ds(0, WINDOW), :], recv_vl.at[j])

        @pl.when(jnp.logical_not(has_left))
        def _():
            kbuf[j, 0:WINDOW, :] = kbuf[j, WINDOW:2 * WINDOW, :]
            vbuf[j, 0:WINDOW, :] = jnp.zeros((WINDOW, HEAD_DIM), jnp.bfloat16)

        @pl.when(has_right)
        def _():
            await_recv(kbuf.at[j, pl.ds(2 * WINDOW, WINDOW), :], recv_kr.at[j])
            await_recv(vbuf.at[j, pl.ds(2 * WINDOW, WINDOW), :], recv_vr.at[j])

        @pl.when(jnp.logical_not(has_right))
        def _():
            kbuf[j, 2 * WINDOW:, :] = kbuf[j, WINDOW:2 * WINDOW, :]
            vbuf[j, 2 * WINDOW:, :] = jnp.zeros((WINDOW, HEAD_DIM), jnp.bfloat16)

    def attend(j):
        await_recv(qbuf.at[j], recv_q.at[j])

        @pl.loop(0, WINDOW // CHUNK)
        def _(c):
            rows = pl.ds(pl.multiple_of(c * CHUNK, CHUNK), CHUNK)
            scores = lax.dot_general(
                qbuf[j, rows, :], kbuf[j], (((1,), (1,)), ((), ())),
                preferred_element_type=jnp.float32,
            )
            top = jnp.max(scores, axis=1, keepdims=True)
            weights = jnp.exp2((scores - top) * SCALE)
            total = (
                left_flag * jnp.sum(weights[:, :WINDOW], axis=1, keepdims=True)
                + jnp.sum(weights[:, WINDOW:2 * WINDOW], axis=1, keepdims=True)
                + right_flag * jnp.sum(weights[:, 2 * WINDOW:], axis=1, keepdims=True)
            )
            mixed = jnp.dot(
                weights.astype(jnp.bfloat16), vbuf[j], preferred_element_type=jnp.float32
            )
            obuf[j, rows, :] = (mixed / total).astype(jnp.bfloat16)

    def give_back(j):
        @pl.loop(0, SHARES)
        def _(i):
            column = pl.multiple_of(site_id * HEAD_DIM, HEAD_DIM)
            row = pl.multiple_of(i * ROWS, 16)
            pltpu.make_async_remote_copy(
                src_ref=obuf.at[j, pl.ds(row, ROWS), :],
                dst_ref=vel.at[j, :, pl.ds(column, HEAD_DIM)],
                send_sem=send_o.at[j],
                recv_sem=recv_o.at[j],
                device_id=(far, i),
                device_id_type=MESH,
            ).start()

    def levels():
        now, change = [], []
        for f in range(FRAMES):
            step = jnp.full((TOKENS, HEAD_DIM), steps_ref[f], jnp.int32)
            level = noise_level(step.astype(jnp.float32))
            level_next = noise_level((step + 1).astype(jnp.float32))
            now.append(level)
            change.append(level_next - level)
        return now, change

    def update(j):
        await_recv(obuf.at[j], recv_o.at[j])
        now, change = levels()
        for i in range(SHARES):
            head = slice((i * CLASSES + j) * HEAD_DIM, (i * CLASSES + j + 1) * HEAD_DIM)
            block = slice(i * HEAD_DIM, (i + 1) * HEAD_DIM)
            speed = vel[j, :, block].astype(jnp.float32)
            latent = lat[:, head].astype(jnp.float32)
            for f in range(FRAMES):
                frame = slice(f * TOKENS, (f + 1) * TOKENS)
                updated = (latent[frame] + change[f] * speed[frame]).astype(jnp.bfloat16)
                den_ref[f, :, head] = (latent[frame] - now[f] * speed[frame]).astype(jnp.bfloat16)
                if f < FRAMES - 1:
                    next_ref[f + 1, :, head] = updated
                else:
                    leave[j, 0:TOKENS, block] = updated

        @pl.when(q < N_QUEUE - 1)
        def _():
            frame_copy(j).start()

    def frame_copy(j):
        return pltpu.make_async_remote_copy(
            src_ref=leave.at[j],
            dst_ref=arrive.at[j],
            send_sem=send_l.at[j],
            recv_sem=recv_l.at[j],
            device_id=((q + 1) % N_QUEUE, h),
            device_id_type=MESH,
        )

    leave[:, TOKENS:, :] = jnp.zeros((CLASSES, PAD - TOKENS, SHARES * HEAD_DIM), jnp.bfloat16)

    scatter_class(0)
    scatter_class(1)
    forward(0)
    scatter_class(2)
    gather_context(0)
    attend(0)
    give_back(0)
    forward(1)
    gather_context(1)
    attend(1)
    give_back(1)
    forward(2)
    lat_copy.wait()
    update(0)
    gather_context(2)
    attend(2)
    give_back(2)
    update(1)
    update(2)

    def fin_copy(i):
        return pltpu.make_async_remote_copy(
            src_ref=fin_stage.at[i],
            dst_ref=fin_land,
            send_sem=send_f,
            recv_sem=recv_f,
            device_id=(i, h),
            device_id_type=MESH,
        )

    @pl.when(q == N_QUEUE - 1)
    def _():
        fin_stage[:, TOKENS:, :] = jnp.zeros((N_QUEUE, PAD - TOKENS, HEAD_DIM), jnp.bfloat16)
        for i in range(SHARES):
            block = slice(i * HEAD_DIM, (i + 1) * HEAD_DIM)
            wide = jnp.concatenate(
                [leave[j, 0:TOKENS, block].astype(jnp.float32) for j in range(CLASSES)], axis=1
            )
            for p in range(4):
                piece = wide[:, p * COLUMNS:(p + 1) * COLUMNS].astype(jnp.bfloat16)
                fin_stage[4 * i + p, 0:TOKENS, 0:COLUMNS] = piece
                fin_stage[4 * i + p, 0:TOKENS, COLUMNS:] = jnp.zeros(
                    (TOKENS, HEAD_DIM - COLUMNS), jnp.bfloat16
                )

        @pl.loop(0, N_QUEUE - 1)
        def _(i):
            fin_copy(i).start()

        fin_ref[...] = fin_stage[N_QUEUE - 1, 0:TOKENS, 0:COLUMNS]

    @pl.when(q == 0)
    def _():
        next_ref[0] = noise_ref[...]

    @pl.when(q > 0)
    def _():
        for j in range(CLASSES):
            frame_copy(j).wait_recv()
            for i in range(SHARES):
                head = slice((i * CLASSES + j) * HEAD_DIM, (i * CLASSES + j + 1) * HEAD_DIM)
                next_ref[0, :, head] = arrive[j, 0:TOKENS, i * HEAD_DIM:(i + 1) * HEAD_DIM]

    @pl.when(q < N_QUEUE - 1)
    def _():
        await_recv(fin_land, recv_f)
        fin_ref[...] = fin_land[0:TOKENS, 0:COLUMNS]

    await_recv(q_hbm, send_q)
    await_recv(k_hbm, send_k)
    await_recv(v_hbm, send_v)
    for j in range(CLASSES):
        await_recv(obuf.at[j], send_o.at[j])

        @pl.when(has_right)
        def _():
            await_recv(own(kbuf, j), send_n.at[0, j])
            await_recv(own(vbuf, j), send_n.at[2, j])

        @pl.when(has_left)
        def _():
            await_recv(own(kbuf, j), send_n.at[1, j])
            await_recv(own(vbuf, j), send_n.at[3, j])

        @pl.when(q < N_QUEUE - 1)
        def _():
            frame_copy(j).wait_send()

    @pl.when(q == N_QUEUE - 1)
    def _():
        await_recv(fin_stage.at[pl.ds(0, N_QUEUE - 1)], send_f)


def shards(latents, queries, key_proj, values, slot_steps, noise_frame):
    def flat(array):
        return array.reshape(ROWS, D)

    anywhere = pl.BlockSpec(memory_space=pl.ANY)
    vmem = pl.BlockSpec(memory_space=pltpu.VMEM)
    bf16 = jnp.bfloat16
    dma = pltpu.SemaphoreType.DMA
    return pl.pallas_call(
        kernel,
        out_shape=(
            jax.ShapeDtypeStruct((FRAMES, TOKENS, D), bf16),
            jax.ShapeDtypeStruct((FRAMES, TOKENS, D), bf16),
            jax.ShapeDtypeStruct((TOKENS, COLUMNS), bf16),
        ),
        in_specs=[anywhere] * 4 + [vmem, pl.BlockSpec(memory_space=pltpu.SMEM)],
        out_specs=(vmem, vmem, vmem),
        scratch_shapes=[
            pltpu.VMEM((CLASSES, WINDOW, HEAD_DIM), bf16),
            pltpu.VMEM((CLASSES, CONTEXT, HEAD_DIM), bf16),
            pltpu.VMEM((CLASSES, CONTEXT, HEAD_DIM), bf16),
            pltpu.VMEM((CLASSES, WINDOW, HEAD_DIM), bf16),
            pltpu.VMEM((CLASSES, ROWS, SHARES * HEAD_DIM), bf16),
            pltpu.VMEM((ROWS, D), bf16),
            pltpu.VMEM((CLASSES, PAD, SHARES * HEAD_DIM), bf16),
            pltpu.VMEM((CLASSES, PAD, SHARES * HEAD_DIM), bf16),
            pltpu.VMEM((N_QUEUE, PAD, HEAD_DIM), bf16),
            pltpu.VMEM((PAD, HEAD_DIM), bf16),
            dma, dma, dma,
            dma((CLASSES,)), dma((CLASSES,)), dma((CLASSES,)),
            dma((4, CLASSES)),
            dma((CLASSES,)), dma((CLASSES,)), dma((CLASSES,)), dma((CLASSES,)),
            dma((CLASSES,)), dma((CLASSES,)),
            dma((CLASSES,)), dma((CLASSES,)),
            dma, dma, dma,
        ],
        compiler_params=pltpu.CompilerParams(
            collective_id=0, has_side_effects=True, vmem_limit_bytes=48 * 1024 * 1024
        ),
    )(flat(queries), flat(key_proj), flat(values), flat(latents), noise_frame, slot_steps)


def solution(mesh):
    spec = P("queue", "head", None)
    return jax.shard_map(
        shards,
        mesh=mesh,
        in_specs=(spec, spec, spec, spec, P("queue"), P("head", None)),
        out_specs=(spec, spec, P("head", "queue")),
        check_vma=False,
    )
```

time: 921 us -> 104 us (0.11); the launches traced: 907 us -> 103 us
  waiting for transfers between devices: 747 us -> 0 us
  Pallas kernels: 0 us -> 94.3 us
  matrix products: 69.7 us -> 0 us
  local copies, waits for them, and re-layouts: 51.3 us -> 8.04 us
  other arithmetic: 14.6 us -> 0 us
  between operations: 14.2 us -> 0.65 us
  starting transfers between devices: 9.8 us -> 0 us
    all_gather x1 -> x0, waiting for transfers between devices: 490 us -> none  [shards(): piece = lax.all_gather(extended, 'head', axis=2, tiled=True)]
    psum x1 -> x0, waiting for transfers between devices: 237 us -> none  [from_root(): return lax.psum(jnp.where(mine, shard, jnp.zeros_like(shard)), axis)]
    pallas_call x0 -> x1, Pallas kernels: none -> 94.3 us  [shards(): pl.pallas_call(kernel, out_shape=(jax.ShapeDtypeStruct((FRAMES, TOKENS, D...]
    dot_general x48 -> x0, matrix products: 69.7 us -> none  [the longest x24 35.9 us: one_head(): jnp.einsum('qd,kd->qk', query_head, key_head, preferred_element_type=jnp....]
    unnamed x18 -> x15, local copies, waits for them, and re-layouts: 33.1 us -> 8.04 us
    ppermute x3 -> x0, waiting for transfers between devices: 20.1 us -> none  [the longest x1 11.9 us: padded(): lax.ppermute(tail, axis, [(i, (i + 1) % count) for i in range(ends)])]
    slice x2 -> x0, local copies, waits for them, and re-layouts: 11.5 us -> none  [the longest x1 11.5 us: shards(): piece[1].reshape(3 * frames * piece_rows, HEADS, HEAD_DIM)]
    ppermute x3 -> x0, starting transfers between devices: 9.72 us -> none  [the longest x1 5.75 us: padded(): lax.ppermute(head, axis, [((i + 1) % count, i) for i in range(ends)])]
  transfers between devices with their start and end apart: 5 -> 0, of which waited for: 5 -> 0; matrix products, arithmetic and copies ran while one was open for 0% -> 0% of each run, Pallas kernels for 0% -> 0%
where the time goes in v1:
time: 104 us; the launch traced here: 103 us
  Pallas kernels  94.3 us (91%)
  local copies, waits for them, and re-layouts  8.04 us (8%)
    pallas_call x1, Pallas kernels, shards(): pl.pallas_call(kernel, out_shape=(jax.ShapeDtypeStruct((FRAMES, TOKENS, D...  94.3 us
    unnamed x15, local copies, waits for them, and re-layouts  8.04 us

profile of v1, /device:TPU:32, one launch (start us, length us, event | category | flops | bytes accessed | tf_op | source)
XLA Modules:
  0.0 102.9 jit_solution(803148633186971186)
XLA Ops:
  0.6 0.0 copy-start.5
  0.6 0.6 copy-done.5
  1.3 0.0 copy-start
  1.3 1.1 %copy-done = bf16[4,24,3072]{2,1,0:T(8,128)(2,1)S(1)} copy-done((bf16[4,24,3072]{2,1,0:T(8,128)(2,1)S(1)}, bf16[4,24,3072]{2,1,0:T(8,128)(2,1)}, u32[]{:S(2)}) %copy-start) | copy-done | bytes 589848
  2.4 0.0 copy-start.1
  2.4 1.1 %copy-done.1 = bf16[4,24,3072]{2,1,0:T(8,128)(2,1)S(1)} copy-done((bf16[4,24,3072]{2,1,0:T(8,128)(2,1)S(1)}, bf16[4,24,3072]{2,1,0:T(8,128)(2,1)}, u32[]{:S(2)}) %copy-start.1) | copy-done | bytes 589848
  3.4 0.0 copy-start.2
  3.4 1.1 %copy-done.2 = bf16[4,24,3072]{2,1,0:T(8,128)(2,1)S(1)} copy-done((bf16[4,24,3072]{2,1,0:T(8,128)(2,1)S(1)}, bf16[4,24,3072]{2,1,0:T(8,128)(2,1)}, u32[]{:S(2)}) %copy-start.2) | copy-done | bytes 589848
  4.5 0.0 copy-start.3
  4.5 1.1 %copy-done.3 = bf16[4,24,3072]{2,1,0:T(8,128)(2,1)S(1)} copy-done((bf16[4,24,3072]{2,1,0:T(8,128)(2,1)S(1)}, bf16[4,24,3072]{2,1,0:T(8,128)(2,1)}, u32[]{:S(2)}) %copy-start.3) | copy-done | bytes 589848
  5.5 0.0 copy-start.4
  5.5 0.9 copy-done.4
  6.5 94.3 %shard_map.85 = (bf16[4,24,3072]{2,1,0:T(8,128)(2,1)S(1)}, bf16[4,24,3072]{2,1,0:T(8,128)(2,1)S(1)}, bf16[24,96]{1,0:T(8,128)(2,1)S(1)}) custom-call(bf16[96,3072]{1,0:T(8,128)(2,1)S(1)} %bitcast.4, bf16[96,3072]{1,0:T(8,128)(2,1)S(1)} %bitcast.5, bf16[96,3072]{1,0:T(8,128)(2,1)S(1)} %bitcast.6, bf16[96,3072]{1,0:T(8,128)(2,1)S(1)} %bitcast.7, ...), custom_call_target="tpu_custom_call" | custom-call | tf_op jit(solution)/shard_map/pallas_call | solution.py:359
  100.7 0.8 copy.12
  101.5 0.8 copy.13
  102.3 0.6 copy.14
Async XLA Ops:
  0.6 0.7 copy-start.5
  1.3 1.1 %copy-start = (bf16[4,24,3072]{2,1,0:T(8,128)(2,1)S(1)}, bf16[4,24,3072]{2,1,0:T(8,128)(2,1)}, u32[]{:S(2)}) copy-start(bf16[4,24,3072]{2,1,0:T(8,128)(2,1)} %param.7) | copy-start | bytes 1769476
  2.4 1.1 %copy-start.1 = (bf16[4,24,3072]{2,1,0:T(8,128)(2,1)S(1)}, bf16[4,24,3072]{2,1,0:T(8,128)(2,1)}, u32[]{:S(2)}) copy-start(bf16[4,24,3072]{2,1,0:T(8,128)(2,1)} %param.8) | copy-start | bytes 1769476
  3.4 1.1 %copy-start.2 = (bf16[4,24,3072]{2,1,0:T(8,128)(2,1)S(1)}, bf16[4,24,3072]{2,1,0:T(8,128)(2,1)}, u32[]{:S(2)}) copy-start(bf16[4,24,3072]{2,1,0:T(8,128)(2,1)} %param.9) | copy-start | bytes 1769476
  4.5 1.1 %copy-start.3 = (bf16[4,24,3072]{2,1,0:T(8,128)(2,1)S(1)}, bf16[4,24,3072]{2,1,0:T(8,128)(2,1)}, u32[]{:S(2)}) copy-start(bf16[4,24,3072]{2,1,0:T(8,128)(2,1)} %param.6) | copy-start | bytes 1769476
  5.5 0.9 copy-start.4

commit v2 on v1

--- a/solution.py
+++ b/solution.py
@@ -22,7 +22,8 @@
 N_QUEUE = 32
 STEPS = 128
 HALF = N_QUEUE // 2
-CHUNK = 256
+CHUNK = 192
+PIECE = WINDOW // 4
 PAD = 32
 COLUMNS = D // N_QUEUE
 SCALE = math.log2(math.e) / math.sqrt(HEAD_DIM)
@@ -35,12 +36,12 @@
 
 
 def kernel(
-    q_hbm, k_hbm, v_hbm, lat_hbm, noise_ref, steps_ref,
+    q_hbm, k_hbm, v_hbm, lat_hbm, noise_hbm, steps_hbm,
     next_ref, den_ref, fin_ref,
-    qbuf, kbuf, vbuf, obuf, vel, lat, leave, arrive, fin_stage, fin_land,
+    qbuf, kbuf, vbuf, obuf, vel, lat, leave, arrive, fin_stage, fin_land, relayed, steps_ref,
     send_q, send_k, send_v, recv_q, recv_k, recv_v,
-    send_n, recv_kl, recv_kr, recv_vl, recv_vr,
-    send_o, recv_o, send_l, recv_l, send_f, recv_f, lat_sem,
+    send_n, recv_n, send_r, recv_r,
+    send_o, recv_o, send_l, recv_l, send_f, recv_f, lat_sem, noise_sem, steps_sem,
 ):
     q = lax.axis_index("queue")
     h = lax.axis_index("head")
@@ -58,13 +59,37 @@
     def site_of(win, ident):
         return ((win + HALF) % N_QUEUE, (ident // 2) * 2 + (ident + flip(win)) % 2)
 
+    group, place = window // 8, window % 8
     has_left = window > 0
     has_right = window < N_QUEUE - 1
+    last = jnp.logical_and(place == 7, has_right)
+    first = jnp.logical_and(place == 0, has_left)
+    plain_right = place < 7
+    plain_left = place > 0
+    up = jnp.logical_and(jnp.logical_and(place % 2 == 1, place < 7), group < 3)
+    down = jnp.logical_and(jnp.logical_and(place % 2 == 0, place > 0), group > 0)
+    is_relay = jnp.logical_or(up, down)
+    relay_from = site_of(jnp.where(up, 8 * group + 7, 8 * group), site_id)
+    relay_to = site_of(jnp.where(up, 8 * group + 8, (8 * group + N_QUEUE - 1) % N_QUEUE) % N_QUEUE, site_id)
+
+    def relay_up(grp, p):
+        return site_of((8 * grp + 2 * p + 1) % N_QUEUE, site_id)
+
+    def relay_down(grp, p):
+        return site_of((8 * grp + 2 * p) % N_QUEUE, site_id)
+
     left_site = site_of((window + N_QUEUE - 1) % N_QUEUE, site_id)
     right_site = site_of((window + 1) % N_QUEUE, site_id)
 
     lat_copy = pltpu.make_async_copy(lat_hbm, lat, lat_sem)
     lat_copy.start()
+    steps_copy = pltpu.make_async_copy(steps_hbm, steps_ref, steps_sem)
+    steps_copy.start()
+    noise_copy = pltpu.make_async_copy(noise_hbm, next_ref.at[0], noise_sem)
+
+    @pl.when(q == 0)
+    def _():
+        noise_copy.start()
 
     barrier = pltpu.get_barrier_semaphore()
 
@@ -83,6 +108,23 @@
     def _():
         greet(right_site)
 
+    @pl.when(last)
+    def _():
+        for p in range(3):
+            greet(relay_up(group, p))
+            greet(relay_down(group + 1, p + 1))
+
+    @pl.when(first)
+    def _():
+        for p in range(3):
+            greet(relay_down(group, p + 1))
+            greet(relay_up(group + 3, p))
+
+    @pl.when(is_relay)
+    def _():
+        greet(relay_from)
+        greet(relay_to)
+
     @pl.when(q > 0)
     def _():
         greet((q - 1, h))
@@ -99,28 +141,34 @@
             greet((i, h))
 
     edges = SHARES + has_left.astype(jnp.int32) + has_right.astype(jnp.int32)
+    edges = edges + 6 * last.astype(jnp.int32) + 6 * first.astype(jnp.int32) + 2 * is_relay.astype(jnp.int32)
     edges = edges + (q > 0).astype(jnp.int32) + 2 * (q < N_QUEUE - 1).astype(jnp.int32)
     edges = edges + (N_QUEUE - 1) * (q == N_QUEUE - 1).astype(jnp.int32)
     pl.semaphore_wait(barrier, edges)
 
     def scatter(src, dst, send, recv, j, row0):
         @pl.loop(0, SHARES)
-        def _(i):
+        def _(n):
+            i = (2 * y + n) % SHARES
             column = pl.multiple_of((i * CLASSES + j) * HEAD_DIM, HEAD_DIM)
             row = pl.multiple_of(row0 + h * ROWS, 16)
             pltpu.make_async_remote_copy(
                 src_ref=src.at[:, pl.ds(column, HEAD_DIM)],
                 dst_ref=dst.at[j, pl.ds(row, ROWS), :],
                 send_sem=send,
-                recv_sem=recv.at[j],
+                recv_sem=recv,
                 device_id=site_of(q, i),
                 device_id_type=MESH,
             ).start()
 
-    def scatter_class(j):
-        scatter(k_hbm, kbuf, send_k, recv_k, j, WINDOW)
-        scatter(v_hbm, vbuf, send_v, recv_v, j, WINDOW)
-        scatter(q_hbm, qbuf, send_q, recv_q, j, 0)
+    def scatter_keys(j):
+        scatter(k_hbm, kbuf, send_k, recv_k.at[j], j, WINDOW)
+
+    def scatter_values(j):
+        scatter(v_hbm, vbuf, send_v, recv_v.at[j], j, WINDOW)
+
+    def scatter_queries(j):
+        scatter(q_hbm, qbuf, send_q, recv_q.at[j, y], j, 0)
 
     def await_recv(ref, sem):
         pltpu.make_async_copy(ref, ref, sem).wait()
@@ -128,29 +176,65 @@
     def own(buf, j):
         return buf.at[j, pl.ds(WINDOW, WINDOW), :]
 
-    def pass_on(buf, j, side, recv, device, slot):
+    def pass_on(n, buf, j, side, device, base, start, rows):
         return pltpu.make_async_remote_copy(
-            src_ref=own(buf, j),
-            dst_ref=buf.at[j, pl.ds(slot * WINDOW, WINDOW), :],
-            send_sem=send_n.at[side, j],
-            recv_sem=recv.at[j],
+            src_ref=buf.at[j, pl.ds(WINDOW + start, rows), :],
+            dst_ref=buf.at[j, pl.ds(base + start, rows), :],
+            send_sem=send_n.at[n, side, j],
+            recv_sem=recv_n.at[n, side, j],
             device_id=device,
             device_id_type=MESH,
         )
 
-    def forward(j):
-        for n, (buf, recv, recv_left, recv_right) in enumerate(
-            ((kbuf, recv_k, recv_kl, recv_kr), (vbuf, recv_v, recv_vl, recv_vr))
-        ):
-            await_recv(own(buf, j), recv.at[j])
-
-            @pl.when(has_right)
-            def _():
-                pass_on(buf, j, 2 * n, recv_left, right_site, 0).start()
-
-            @pl.when(has_left)
-            def _():
-                pass_on(buf, j, 2 * n + 1, recv_right, left_site, 2).start()
+    def by_relay(n, buf, j, side, device, start):
+        return pltpu.make_async_remote_copy(
+            src_ref=buf.at[j, pl.ds(WINDOW + start, PIECE), :],
+            dst_ref=relayed.at[n, j],
+            send_sem=send_n.at[n, side, j],
+            recv_sem=recv_r.at[n, j],
+            device_id=device,
+            device_id_type=MESH,
+        )
+
+    def forward(n, j):
+        buf, recv = ((kbuf, recv_k), (vbuf, recv_v))[n]
+        await_recv(own(buf, j), recv.at[j])
+
+        @pl.when(plain_right)
+        def _():
+            pass_on(n, buf, j, 0, right_site, 0, 0, WINDOW).start()
+
+        @pl.when(plain_left)
+        def _():
+            pass_on(n, buf, j, 1, left_site, 2 * WINDOW, 0, WINDOW).start()
+
+        @pl.when(last)
+        def _():
+            pass_on(n, buf, j, 0, right_site, 0, 3 * PIECE, PIECE).start()
+            for p in range(3):
+                by_relay(n, buf, j, 0, relay_up(group, p), p * PIECE).start()
+
+        @pl.when(first)
+        def _():
+            pass_on(n, buf, j, 1, left_site, 2 * WINDOW, 0, PIECE).start()
+            for p in range(3):
+                by_relay(n, buf, j, 1, relay_down(group, p + 1), (p + 1) * PIECE).start()
+
+    def relay(j):
+        @pl.when(is_relay)
+        def _():
+            side = jnp.where(up, 0, 1)
+            row = pl.multiple_of(jnp.where(up, 0, 2 * WINDOW) + place // 2 * PIECE, 16)
+            for n, buf in enumerate((kbuf, vbuf)):
+                await_recv(relayed.at[n, j], recv_r.at[n, j])
+                pltpu.make_async_remote_copy(
+                    src_ref=relayed.at[n, j],
+                    dst_ref=buf.at[j, pl.ds(row, PIECE), :],
+                    send_sem=send_r.at[n, j],
+                    recv_sem=recv_n.at[n, side, j],
+                    device_id=relay_to,
+                    device_id_type=MESH,
+                ).start()
 
     left_flag = has_left.astype(jnp.float32)
     right_flag = has_right.astype(jnp.float32)
@@ -158,8 +242,8 @@
     def gather_context(j):
         @pl.when(has_left)
         def _():
-            await_recv(kbuf.at[j, pl.ds(0, WINDOW), :], recv_kl.at[j])
-            await_recv(vbuf.at[j, pl.ds(0, WINDOW), :], recv_vl.at[j])
+            await_recv(kbuf.at[j, pl.ds(0, WINDOW), :], recv_n.at[0, 0, j])
+            await_recv(vbuf.at[j, pl.ds(0, WINDOW), :], recv_n.at[1, 0, j])
 
         @pl.when(jnp.logical_not(has_left))
         def _():
@@ -168,8 +252,8 @@
 
         @pl.when(has_right)
         def _():
-            await_recv(kbuf.at[j, pl.ds(2 * WINDOW, WINDOW), :], recv_kr.at[j])
-            await_recv(vbuf.at[j, pl.ds(2 * WINDOW, WINDOW), :], recv_vr.at[j])
+            await_recv(kbuf.at[j, pl.ds(2 * WINDOW, WINDOW), :], recv_n.at[0, 1, j])
+            await_recv(vbuf.at[j, pl.ds(2 * WINDOW, WINDOW), :], recv_n.at[1, 1, j])
 
         @pl.when(jnp.logical_not(has_right))
         def _():
@@ -177,11 +261,11 @@
             vbuf[j, 2 * WINDOW:, :] = jnp.zeros((WINDOW, HEAD_DIM), jnp.bfloat16)
 
     def attend(j):
-        await_recv(qbuf.at[j], recv_q.at[j])
-
         @pl.loop(0, WINDOW // CHUNK)
-        def _(c):
+        def _(n):
+            c = (y + n) % (WINDOW // CHUNK)
             rows = pl.ds(pl.multiple_of(c * CHUNK, CHUNK), CHUNK)
+            await_recv(qbuf.at[j, rows, :], recv_q.at[j, c])
             scores = lax.dot_general(
                 qbuf[j, rows, :], kbuf[j], (((1,), (1,)), ((), ())),
                 preferred_element_type=jnp.float32,
@@ -198,19 +282,20 @@
             )
             obuf[j, rows, :] = (mixed / total).astype(jnp.bfloat16)
 
-    def give_back(j):
-        @pl.loop(0, SHARES)
-        def _(i):
-            column = pl.multiple_of(site_id * HEAD_DIM, HEAD_DIM)
-            row = pl.multiple_of(i * ROWS, 16)
-            pltpu.make_async_remote_copy(
-                src_ref=obuf.at[j, pl.ds(row, ROWS), :],
-                dst_ref=vel.at[j, :, pl.ds(column, HEAD_DIM)],
-                send_sem=send_o.at[j],
-                recv_sem=recv_o.at[j],
-                device_id=(far, i),
-                device_id_type=MESH,
-            ).start()
+            for i in range(CHUNK // ROWS):
+                give_back(j, c * (CHUNK // ROWS) + i)
+
+    def give_back(j, i):
+        column = pl.multiple_of(site_id * HEAD_DIM, HEAD_DIM)
+        row = pl.multiple_of(i * ROWS, 16)
+        pltpu.make_async_remote_copy(
+            src_ref=obuf.at[j, pl.ds(row, ROWS), :],
+            dst_ref=vel.at[j, :, pl.ds(column, HEAD_DIM)],
+            send_sem=send_o.at[j],
+            recv_sem=recv_o.at[j],
+            device_id=(far, i),
+            device_id_type=MESH,
+        ).start()
 
     def levels():
         now, change = [], []
@@ -255,23 +340,33 @@
 
     leave[:, TOKENS:, :] = jnp.zeros((CLASSES, PAD - TOKENS, SHARES * HEAD_DIM), jnp.bfloat16)
 
-    scatter_class(0)
-    scatter_class(1)
-    forward(0)
-    scatter_class(2)
+    scatter_keys(0)
+    scatter_values(0)
+    scatter_keys(1)
+    scatter_values(1)
+    forward(0, 0)
+    scatter_queries(0)
+    forward(1, 0)
+    scatter_keys(2)
+    relay(0)
+    forward(0, 1)
+    scatter_values(2)
+    forward(1, 1)
+    scatter_queries(1)
+    relay(1)
+    scatter_queries(2)
     gather_context(0)
     attend(0)
-    give_back(0)
-    forward(1)
+    forward(0, 2)
+    forward(1, 2)
+    relay(2)
     gather_context(1)
     attend(1)
-    give_back(1)
-    forward(2)
     lat_copy.wait()
+    steps_copy.wait()
     update(0)
     gather_context(2)
     attend(2)
-    give_back(2)
     update(1)
     update(2)
 
@@ -308,7 +403,7 @@
 
     @pl.when(q == 0)
     def _():
-        next_ref[0] = noise_ref[...]
+        noise_copy.wait()
 
     @pl.when(q > 0)
     def _():
@@ -331,13 +426,18 @@
 
         @pl.when(has_right)
         def _():
-            await_recv(own(kbuf, j), send_n.at[0, j])
-            await_recv(own(vbuf, j), send_n.at[2, j])
+            await_recv(own(kbuf, j), send_n.at[0, 0, j])
+            await_recv(own(vbuf, j), send_n.at[1, 0, j])
 
         @pl.when(has_left)
         def _():
-            await_recv(own(kbuf, j), send_n.at[1, j])
-            await_recv(own(vbuf, j), send_n.at[3, j])
+            await_recv(own(kbuf, j), send_n.at[0, 1, j])
+            await_recv(own(vbuf, j), send_n.at[1, 1, j])
+
+        @pl.when(is_relay)
+        def _():
+            await_recv(relayed.at[0, j], send_r.at[0, j])
+            await_recv(relayed.at[1, j], send_r.at[1, j])
 
         @pl.when(q < N_QUEUE - 1)
         def _():
@@ -352,7 +452,7 @@
     def flat(array):
         return array.reshape(ROWS, D)
 
-    anywhere = pl.BlockSpec(memory_space=pl.ANY)
+    hbm = pl.BlockSpec(memory_space=pltpu.HBM)
     vmem = pl.BlockSpec(memory_space=pltpu.VMEM)
     bf16 = jnp.bfloat16
     dma = pltpu.SemaphoreType.DMA
@@ -363,7 +463,7 @@
             jax.ShapeDtypeStruct((FRAMES, TOKENS, D), bf16),
             jax.ShapeDtypeStruct((TOKENS, COLUMNS), bf16),
         ),
-        in_specs=[anywhere] * 4 + [vmem, pl.BlockSpec(memory_space=pltpu.SMEM)],
+        in_specs=[hbm] * 6,
         out_specs=(vmem, vmem, vmem),
         scratch_shapes=[
             pltpu.VMEM((CLASSES, WINDOW, HEAD_DIM), bf16),
@@ -376,18 +476,19 @@
             pltpu.VMEM((CLASSES, PAD, SHARES * HEAD_DIM), bf16),
             pltpu.VMEM((N_QUEUE, PAD, HEAD_DIM), bf16),
             pltpu.VMEM((PAD, HEAD_DIM), bf16),
+            pltpu.VMEM((2, CLASSES, PIECE, HEAD_DIM), bf16),
+            pltpu.SMEM((FRAMES,), jnp.int32),
             dma, dma, dma,
-            dma((CLASSES,)), dma((CLASSES,)), dma((CLASSES,)),
-            dma((4, CLASSES)),
-            dma((CLASSES,)), dma((CLASSES,)), dma((CLASSES,)), dma((CLASSES,)),
+            dma((CLASSES, WINDOW // CHUNK)), dma((CLASSES,)), dma((CLASSES,)),
+            dma((2, 2, CLASSES)), dma((2, 2, CLASSES)), dma((2, CLASSES)), dma((2, CLASSES)),
             dma((CLASSES,)), dma((CLASSES,)),
             dma((CLASSES,)), dma((CLASSES,)),
-            dma, dma, dma,
+            dma, dma, dma, dma, dma,
         ],
         compiler_params=pltpu.CompilerParams(
             collective_id=0, has_side_effects=True, vmem_limit_bytes=48 * 1024 * 1024
         ),
-    )(flat(queries), flat(key_proj), flat(values), flat(latents), noise_frame, slot_steps)
+    )(*(pltpu.with_memory_space_constraint(a, pltpu.HBM) for a in (flat(queries), flat(key_proj), flat(values), flat(latents), noise_frame, slot_steps)))
 
 
 def solution(mesh):

time: 104 us -> 76.1 us (0.73)
  Pallas kernels: 94.3 us -> 73.1 us
  local copies, waits for them, and re-layouts: 8.04 us -> 2.22 us
    pallas_call x1, Pallas kernels: 94.3 us -> 73.1 us  [shards(): pl.pallas_call(kernel, out_shape=(jax.ShapeDtypeStruct((FRAMES, TOKENS, D...]
    unnamed x15 -> x3, local copies, waits for them, and re-layouts: 8.04 us -> 2.22 us
where the time goes in v2:
time: 76.1 us; the launch traced here: 76 us
  Pallas kernels  73.1 us (96%)
  local copies, waits for them, and re-layouts  2.22 us (3%)
    pallas_call x1, Pallas kernels, shards(): pl.pallas_call(kernel, out_shape=(jax.ShapeDtypeStruct((FRAMES, TOKENS, D...  73.1 us
    unnamed x3, local copies, waits for them, and re-layouts  2.22 us

profile of v2, /device:TPU:32, one launch (start us, length us, event | category | flops | bytes accessed | tf_op | source)
XLA Modules:
  0.0 76.0 jit_solution(7198277999748674209)
XLA Ops:
  0.6 73.1 %shard_map.85 = (bf16[4,24,3072]{2,1,0:T(8,128)(2,1)S(1)}, bf16[4,24,3072]{2,1,0:T(8,128)(2,1)S(1)}, bf16[24,96]{1,0:T(8,128)(2,1)S(1)}) custom-call(bf16[96,3072]{1,0:T(8,128)(2,1)} %bitcast.4, bf16[96,3072]{1,0:T(8,128)(2,1)} %bitcast.5, bf16[96,3072]{1,0:T(8,128)(2,1)} %bitcast.6, bf16[96,3072]{1,0:T(8,128)(2,1)} %bitcast.7, bf16[24,3072]{1,0:T(8,128)(2,1)} %noise_hbm.1, ...), custom_call_target="tpu_custom_call" | custom-call | tf_op jit(solution)/shard_map/pallas_call | solution.py:459
  73.8 0.8 %copy.12 = bf16[4,24,3072]{2,1,0:T(8,128)(2,1)} copy(bf16[4,24,3072]{2,1,0:T(8,128)(2,1)S(1)} %get-tuple-element.6) | data formatting | bytes 1179648
  74.6 0.8 %copy.13 = bf16[4,24,3072]{2,1,0:T(8,128)(2,1)} copy(bf16[4,24,3072]{2,1,0:T(8,128)(2,1)S(1)} %get-tuple-element.7) | data formatting | bytes 1179648
  75.4 0.6 copy.14

commit v3 on v2

--- a/solution.py
+++ b/solution.py
@@ -25,6 +25,9 @@
 CHUNK = 192
 PIECE = WINDOW // 4
 PAD = 32
+REST = ROWS - PAD
+LAST = CLASSES - 1
+AHEAD = SHARES * PAD
 COLUMNS = D // N_QUEUE
 SCALE = math.log2(math.e) / math.sqrt(HEAD_DIM)
 shift_factor = 3.0
@@ -168,7 +171,25 @@
         scatter(v_hbm, vbuf, send_v, recv_v.at[j], j, WINDOW)
 
     def scatter_queries(j):
-        scatter(q_hbm, qbuf, send_q, recv_q.at[j, y], j, 0)
+        if j < LAST:
+            scatter(q_hbm, qbuf, send_q, recv_q.at[j, y], j, 0)
+            return
+        for rows, start, place_of, sem in (
+            (PAD, REST, h * PAD, recv_q.at[j, 0]),
+            (REST, 0, AHEAD + h * REST, recv_q.at[j, 1 + h // 4]),
+        ):
+            @pl.loop(0, SHARES)
+            def _(n):
+                i = (2 * y + n) % SHARES
+                column = pl.multiple_of((i * CLASSES + j) * HEAD_DIM, HEAD_DIM)
+                pltpu.make_async_remote_copy(
+                    src_ref=q_hbm.at[pl.ds(start, rows), pl.ds(column, HEAD_DIM)],
+                    dst_ref=qbuf.at[j, pl.ds(pl.multiple_of(place_of, 16), rows), :],
+                    send_sem=send_q,
+                    recv_sem=sem,
+                    device_id=site_of(q, i),
+                    device_id_type=MESH,
+                ).start()
 
     def await_recv(ref, sem):
         pltpu.make_async_copy(ref, ref, sem).wait()
@@ -220,21 +241,22 @@
             for p in range(3):
                 by_relay(n, buf, j, 1, relay_down(group, p + 1), (p + 1) * PIECE).start()
 
-    def relay(j):
+    def relay(n, j):
+        buf = (kbuf, vbuf)[n]
+
         @pl.when(is_relay)
         def _():
             side = jnp.where(up, 0, 1)
             row = pl.multiple_of(jnp.where(up, 0, 2 * WINDOW) + place // 2 * PIECE, 16)
-            for n, buf in enumerate((kbuf, vbuf)):
-                await_recv(relayed.at[n, j], recv_r.at[n, j])
-                pltpu.make_async_remote_copy(
-                    src_ref=relayed.at[n, j],
-                    dst_ref=buf.at[j, pl.ds(row, PIECE), :],
-                    send_sem=send_r.at[n, j],
-                    recv_sem=recv_n.at[n, side, j],
-                    device_id=relay_to,
-                    device_id_type=MESH,
-                ).start()
+            await_recv(relayed.at[n, j], recv_r.at[n, j])
+            pltpu.make_async_remote_copy(
+                src_ref=relayed.at[n, j],
+                dst_ref=buf.at[j, pl.ds(row, PIECE), :],
+                send_sem=send_r.at[n, j],
+                recv_sem=recv_n.at[n, side, j],
+                device_id=relay_to,
+                device_id_type=MESH,
+            ).start()
 
     left_flag = has_left.astype(jnp.float32)
     right_flag = has_right.astype(jnp.float32)
@@ -260,40 +282,63 @@
             kbuf[j, 2 * WINDOW:, :] = kbuf[j, WINDOW:2 * WINDOW, :]
             vbuf[j, 2 * WINDOW:, :] = jnp.zeros((WINDOW, HEAD_DIM), jnp.bfloat16)
 
+    def attend_rows(j, rows):
+        scores = lax.dot_general(
+            qbuf[j, rows, :], kbuf[j], (((1,), (1,)), ((), ())),
+            preferred_element_type=jnp.float32,
+        )
+        top = jnp.max(scores, axis=1, keepdims=True)
+        weights = jnp.exp2((scores - top) * SCALE)
+        total = (
+            left_flag * jnp.sum(weights[:, :WINDOW], axis=1, keepdims=True)
+            + jnp.sum(weights[:, WINDOW:2 * WINDOW], axis=1, keepdims=True)
+            + right_flag * jnp.sum(weights[:, 2 * WINDOW:], axis=1, keepdims=True)
+        )
+        mixed = jnp.dot(
+            weights.astype(jnp.bfloat16), vbuf[j], preferred_element_type=jnp.float32
+        )
+        obuf[j, rows, :] = (mixed / total).astype(jnp.bfloat16)
+
     def attend(j):
-        @pl.loop(0, WINDOW // CHUNK)
+        if j < LAST:
+            @pl.loop(0, WINDOW // CHUNK)
+            def _(n):
+                c = (y + n) % (WINDOW // CHUNK)
+                rows = pl.ds(pl.multiple_of(c * CHUNK, CHUNK), CHUNK)
+                await_recv(qbuf.at[j, rows, :], recv_q.at[j, c])
+                attend_rows(j, rows)
+                for i in range(CHUNK // ROWS):
+                    share = c * (CHUNK // ROWS) + i
+                    give_back(j, share, pl.multiple_of(share * ROWS, 16), 0, ROWS, 0)
+            return
+
+        ahead = pl.ds(0, AHEAD)
+        await_recv(qbuf.at[j, ahead, :], recv_q.at[j, 0])
+        attend_rows(j, ahead)
+
+        @pl.loop(0, SHARES)
         def _(n):
-            c = (y + n) % (WINDOW // CHUNK)
-            rows = pl.ds(pl.multiple_of(c * CHUNK, CHUNK), CHUNK)
-            await_recv(qbuf.at[j, rows, :], recv_q.at[j, c])
-            scores = lax.dot_general(
-                qbuf[j, rows, :], kbuf[j], (((1,), (1,)), ((), ())),
-                preferred_element_type=jnp.float32,
-            )
-            top = jnp.max(scores, axis=1, keepdims=True)
-            weights = jnp.exp2((scores - top) * SCALE)
-            total = (
-                left_flag * jnp.sum(weights[:, :WINDOW], axis=1, keepdims=True)
-                + jnp.sum(weights[:, WINDOW:2 * WINDOW], axis=1, keepdims=True)
-                + right_flag * jnp.sum(weights[:, 2 * WINDOW:], axis=1, keepdims=True)
-            )
-            mixed = jnp.dot(
-                weights.astype(jnp.bfloat16), vbuf[j], preferred_element_type=jnp.float32
-            )
-            obuf[j, rows, :] = (mixed / total).astype(jnp.bfloat16)
-
-            for i in range(CHUNK // ROWS):
-                give_back(j, c * (CHUNK // ROWS) + i)
-
-    def give_back(j, i):
+            share = (2 * y + n) % SHARES
+            give_back(j, share, pl.multiple_of(share * PAD, 16), REST, PAD, 0)
+
+        @pl.loop(0, 2)
+        def _(n):
+            c = (y // 2 + n) % 2
+            rows = pl.ds(pl.multiple_of(AHEAD + c * 4 * REST, 16), 4 * REST)
+            await_recv(qbuf.at[j, rows, :], recv_q.at[j, 1 + c])
+            attend_rows(j, rows)
+            for i in range(4):
+                share = 4 * c + i
+                give_back(j, share, pl.multiple_of(AHEAD + share * REST, 16), 0, REST, 1)
+
+    def give_back(j, share, row, start, rows, part):
         column = pl.multiple_of(site_id * HEAD_DIM, HEAD_DIM)
-        row = pl.multiple_of(i * ROWS, 16)
         pltpu.make_async_remote_copy(
-            src_ref=obuf.at[j, pl.ds(row, ROWS), :],
-            dst_ref=vel.at[j, :, pl.ds(column, HEAD_DIM)],
+            src_ref=obuf.at[j, pl.ds(row, rows), :],
+            dst_ref=vel.at[j, pl.ds(start, rows), pl.ds(column, HEAD_DIM)],
             send_sem=send_o.at[j],
-            recv_sem=recv_o.at[j],
-            device_id=(far, i),
+            recv_sem=recv_o.at[j + part],
+            device_id=(far, share),
             device_id_type=MESH,
         ).start()
 
@@ -307,16 +352,16 @@
             change.append(level_next - level)
         return now, change
 
-    def update(j):
-        await_recv(obuf.at[j], recv_o.at[j])
+    def update(j, frames):
         now, change = levels()
         for i in range(SHARES):
             head = slice((i * CLASSES + j) * HEAD_DIM, (i * CLASSES + j + 1) * HEAD_DIM)
             block = slice(i * HEAD_DIM, (i + 1) * HEAD_DIM)
-            speed = vel[j, :, block].astype(jnp.float32)
-            latent = lat[:, head].astype(jnp.float32)
-            for f in range(FRAMES):
-                frame = slice(f * TOKENS, (f + 1) * TOKENS)
+            base = REST if min(frames) == FRAMES - 1 else 0
+            speed = vel[j, base:, block].astype(jnp.float32)
+            latent = lat[base:, head].astype(jnp.float32)
+            for f in frames:
+                frame = slice(f * TOKENS - base, (f + 1) * TOKENS - base)
                 updated = (latent[frame] + change[f] * speed[frame]).astype(jnp.bfloat16)
                 den_ref[f, :, head] = (latent[frame] - now[f] * speed[frame]).astype(jnp.bfloat16)
                 if f < FRAMES - 1:
@@ -324,9 +369,22 @@
                 else:
                     leave[j, 0:TOKENS, block] = updated
 
-        @pl.when(q < N_QUEUE - 1)
-        def _():
-            frame_copy(j).start()
+        if FRAMES - 1 in frames:
+            @pl.when(q < N_QUEUE - 1)
+            def _():
+                frame_copy(j).start()
+
+    def update_whole(j):
+        await_recv(obuf.at[j], recv_o.at[j])
+        update(j, range(FRAMES))
+
+    def update_ahead():
+        await_recv(obuf.at[LAST, pl.ds(0, AHEAD), :], recv_o.at[LAST])
+        update(LAST, (FRAMES - 1,))
+
+    def update_rest():
+        await_recv(obuf.at[LAST, pl.ds(AHEAD, WINDOW - AHEAD), :], recv_o.at[LAST + 1])
+        update(LAST, range(FRAMES - 1))
 
     def frame_copy(j):
         return pltpu.make_async_remote_copy(
@@ -348,27 +406,31 @@
     scatter_queries(0)
     forward(1, 0)
     scatter_keys(2)
-    relay(0)
+    relay(0, 0)
+    relay(1, 0)
     forward(0, 1)
     scatter_values(2)
+    relay(0, 1)
     forward(1, 1)
     scatter_queries(1)
-    relay(1)
-    scatter_queries(2)
+    relay(1, 1)
     gather_context(0)
     attend(0)
     forward(0, 2)
+    relay(0, 2)
     forward(1, 2)
-    relay(2)
+    scatter_queries(2)
+    relay(1, 2)
     gather_context(1)
     attend(1)
     lat_copy.wait()
     steps_copy.wait()
-    update(0)
+    update_whole(0)
     gather_context(2)
     attend(2)
-    update(1)
-    update(2)
+    update_whole(1)
+
+    update_ahead()
 
     def fin_copy(i):
         return pltpu.make_async_remote_copy(
@@ -400,6 +462,8 @@
             fin_copy(i).start()
 
         fin_ref[...] = fin_stage[N_QUEUE - 1, 0:TOKENS, 0:COLUMNS]
+
+    update_rest()
 
     @pl.when(q == 0)
     def _():
@@ -481,7 +545,7 @@
             dma, dma, dma,
             dma((CLASSES, WINDOW // CHUNK)), dma((CLASSES,)), dma((CLASSES,)),
             dma((2, 2, CLASSES)), dma((2, 2, CLASSES)), dma((2, CLASSES)), dma((2, CLASSES)),
-            dma((CLASSES,)), dma((CLASSES,)),
+            dma((CLASSES,)), dma((CLASSES + 1,)),
             dma((CLASSES,)), dma((CLASSES,)),
             dma, dma, dma, dma, dma,
         ],

time: 76.1 us -> 73.8 us (0.970)
  Pallas kernels: 73.1 us -> 70.8 us
    pallas_call x1, Pallas kernels: 73.1 us -> 70.8 us  [shards(): pl.pallas_call(kernel, out_shape=(jax.ShapeDtypeStruct((FRAMES, TOKENS, D...]
where the time goes in v3:
time: 73.8 us; the launch traced here: 73.7 us
  Pallas kernels  70.8 us (96%)
  local copies, waits for them, and re-layouts  2.22 us (3%)
    pallas_call x1, Pallas kernels, shards(): pl.pallas_call(kernel, out_shape=(jax.ShapeDtypeStruct((FRAMES, TOKENS, D...  70.8 us
    unnamed x3, local copies, waits for them, and re-layouts  2.22 us

profile of v3, /device:TPU:32, one launch (start us, length us, event | category | flops | bytes accessed | tf_op | source)
XLA Modules:
  0.0 73.7 jit_solution(15578746687415526366)
XLA Ops:
  0.6 70.8 %shard_map.85 = (bf16[4,24,3072]{2,1,0:T(8,128)(2,1)S(1)}, bf16[4,24,3072]{2,1,0:T(8,128)(2,1)S(1)}, bf16[24,96]{1,0:T(8,128)(2,1)S(1)}) custom-call(bf16[96,3072]{1,0:T(8,128)(2,1)} %bitcast.4, bf16[96,3072]{1,0:T(8,128)(2,1)} %bitcast.5, bf16[96,3072]{1,0:T(8,128)(2,1)} %bitcast.6, bf16[96,3072]{1,0:T(8,128)(2,1)} %bitcast.7, bf16[24,3072]{1,0:T(8,128)(2,1)} %noise_hbm.1, ...), custom_call_target="tpu_custom_call" | custom-call | tf_op jit(solution)/shard_map/pallas_call | solution.py:523
  71.5 0.8 %copy.12 = bf16[4,24,3072]{2,1,0:T(8,128)(2,1)} copy(bf16[4,24,3072]{2,1,0:T(8,128)(2,1)S(1)} %get-tuple-element.6) | data formatting | bytes 1179648
  72.3 0.8 %copy.13 = bf16[4,24,3072]{2,1,0:T(8,128)(2,1)} copy(bf16[4,24,3072]{2,1,0:T(8,128)(2,1)S(1)} %get-tuple-element.7) | data formatting | bytes 1179648
  73.1 0.6 copy.14

commit v4 on v3

--- a/solution.py
+++ b/solution.py
@@ -114,19 +114,16 @@
     @pl.when(last)
     def _():
         for p in range(3):
-            greet(relay_up(group, p))
             greet(relay_down(group + 1, p + 1))
 
     @pl.when(first)
     def _():
         for p in range(3):
-            greet(relay_down(group, p + 1))
             greet(relay_up(group + 3, p))
 
     @pl.when(is_relay)
     def _():
         greet(relay_from)
-        greet(relay_to)
 
     @pl.when(q > 0)
     def _():
@@ -134,18 +131,11 @@
 
     @pl.when(q < N_QUEUE - 1)
     def _():
-        greet((q + 1, h))
         greet((N_QUEUE - 1, h))
 
-    @pl.when(q == N_QUEUE - 1)
-    def _():
-        @pl.loop(0, N_QUEUE - 1)
-        def _(i):
-            greet((i, h))
-
     edges = SHARES + has_left.astype(jnp.int32) + has_right.astype(jnp.int32)
-    edges = edges + 6 * last.astype(jnp.int32) + 6 * first.astype(jnp.int32) + 2 * is_relay.astype(jnp.int32)
-    edges = edges + (q > 0).astype(jnp.int32) + 2 * (q < N_QUEUE - 1).astype(jnp.int32)
+    edges = edges + 3 * last.astype(jnp.int32) + 3 * first.astype(jnp.int32) + is_relay.astype(jnp.int32)
+    edges = edges + (q < N_QUEUE - 1).astype(jnp.int32)
     edges = edges + (N_QUEUE - 1) * (q == N_QUEUE - 1).astype(jnp.int32)
     pl.semaphore_wait(barrier, edges)
 
@@ -512,6 +502,17 @@
         await_recv(fin_stage.at[pl.ds(0, N_QUEUE - 1)], send_f)
 
 
+def place(next_in, den_in, fin_in, next_out, den_out, fin_out, sems):
+    copies = [
+        pltpu.make_async_copy(source, target, sems.at[n])
+        for n, (source, target) in enumerate(((next_in, next_out), (den_in, den_out), (fin_in, fin_out)))
+    ]
+    for copy in copies:
+        copy.start()
+    for copy in copies:
+        copy.wait()
+
+
 def shards(latents, queries, key_proj, values, slot_steps, noise_frame):
     def flat(array):
         return array.reshape(ROWS, D)
@@ -520,7 +521,7 @@
     vmem = pl.BlockSpec(memory_space=pltpu.VMEM)
     bf16 = jnp.bfloat16
     dma = pltpu.SemaphoreType.DMA
-    return pl.pallas_call(
+    results = pl.pallas_call(
         kernel,
         out_shape=(
             jax.ShapeDtypeStruct((FRAMES, TOKENS, D), bf16),
@@ -555,6 +556,16 @@
     )(*(pltpu.with_memory_space_constraint(a, pltpu.HBM) for a in (flat(queries), flat(key_proj), flat(values), flat(latents), noise_frame, slot_steps)))
 
 
+    anywhere = pl.BlockSpec(memory_space=pl.ANY)
+    return pl.pallas_call(
+        place,
+        out_shape=tuple(jax.ShapeDtypeStruct(r.shape, r.dtype) for r in results),
+        in_specs=[vmem] * 3,
+        out_specs=(anywhere,) * 3,
+        scratch_shapes=[dma((3,))],
+    )(*(pltpu.with_memory_space_constraint(r, pltpu.VMEM) for r in results))
+
+
 def solution(mesh):
     spec = P("queue", "head", None)
     return jax.shard_map(

time: 73.8 us -> 72.2 us (0.978)
  local copies, waits for them, and re-layouts: 2.22 us -> 0 us
    unnamed x3 -> x0, local copies, waits for them, and re-layouts: 2.22 us -> none
    pallas_call x0 -> x1, Pallas kernels: none -> 1.04 us  [shards(): pl.pallas_call(place, out_shape=tuple((jax.ShapeDtypeStruct(r.shape, r.dt...]
where the time goes in v4:
time: 72.2 us
  Pallas kernels  71.5 us (99%)
    pallas_call x1, Pallas kernels, shards(): pl.pallas_call(kernel, out_shape=(jax.ShapeDtypeStruct((FRAMES, TOKENS, D...  70.5 us

profile of v4, /device:TPU:32, one launch (start us, length us, event | category | flops | bytes accessed | tf_op | source)
XLA Modules:
  0.0 72.2 jit_solution(3433087871962641251)
XLA Ops:
  0.6 70.5 %shard_map.85 = (bf16[4,24,3072]{2,1,0:T(8,128)(2,1)S(1)}, bf16[4,24,3072]{2,1,0:T(8,128)(2,1)S(1)}, bf16[24,96]{1,0:T(8,128)(2,1)S(1)}) custom-call(bf16[96,3072]{1,0:T(8,128)(2,1)} %bitcast.4, bf16[96,3072]{1,0:T(8,128)(2,1)} %bitcast.5, bf16[96,3072]{1,0:T(8,128)(2,1)} %bitcast.6, bf16[96,3072]{1,0:T(8,128)(2,1)} %bitcast.7, bf16[24,3072]{1,0:T(8,128)(2,1)} %noise_hbm.1, ...), custom_call_target="tpu_custom_call" | custom-call | tf_op jit(solution)/shard_map/pallas_call | solution.py:524
  71.1 1.0 %shard_map.86 = (bf16[4,24,3072]{2,1,0:T(8,128)(2,1)}, bf16[4,24,3072]{2,1,0:T(8,128)(2,1)}, bf16[24,96]{1,0:T(8,128)(2,1)}) custom-call(bf16[4,24,3072]{2,1,0:T(8,128)(2,1)S(1)} %get-tuple-element.6.next_in, bf16[4,24,3072]{2,1,0:T(8,128)(2,1)S(1)} %get-tuple-element.7.den_in, bf16[24,96]{1,0:T(8,128)(2,1)S(1)} %get-tuple-element.8.fin_in), custom_call_target="tpu_custom_call" | custom-call | tf_op jit(solution)/shard_map/pallas_call | solution.py:560

commit v5 on v4

--- a/solution.py
+++ b/solution.py
@@ -453,19 +453,23 @@
 
         fin_ref[...] = fin_stage[N_QUEUE - 1, 0:TOKENS, 0:COLUMNS]
 
+    def take_frame(classes):
+        @pl.when(q > 0)
+        def _():
+            for j in classes:
+                frame_copy(j).wait_recv()
+                for i in range(SHARES):
+                    head = slice((i * CLASSES + j) * HEAD_DIM, (i * CLASSES + j + 1) * HEAD_DIM)
+                    next_ref[0, :, head] = arrive[j, 0:TOKENS, i * HEAD_DIM:(i + 1) * HEAD_DIM]
+
+    take_frame(range(LAST))
     update_rest()
 
     @pl.when(q == 0)
     def _():
         noise_copy.wait()
 
-    @pl.when(q > 0)
-    def _():
-        for j in range(CLASSES):
-            frame_copy(j).wait_recv()
-            for i in range(SHARES):
-                head = slice((i * CLASSES + j) * HEAD_DIM, (i * CLASSES + j + 1) * HEAD_DIM)
-                next_ref[0, :, head] = arrive[j, 0:TOKENS, i * HEAD_DIM:(i + 1) * HEAD_DIM]
+    take_frame((LAST,))
 
     @pl.when(q < N_QUEUE - 1)
     def _():

time: 72.2 us -> 72.2 us (level)
  no operation moved by 1% of the time
where the time goes in v5:
time: 72.2 us
  Pallas kernels  71.5 us (99%)
    pallas_call x1, Pallas kernels, shards(): pl.pallas_call(kernel, out_shape=(jax.ShapeDtypeStruct((FRAMES, TOKENS, D...  70.5 us

profile of v5, /device:TPU:32, one launch (start us, length us, event | category | flops | bytes accessed | tf_op | source)
XLA Modules:
  0.0 72.2 jit_solution(17053142816263535318)
XLA Ops:
  0.6 70.5 %shard_map.85 = (bf16[4,24,3072]{2,1,0:T(8,128)(2,1)S(1)}, bf16[4,24,3072]{2,1,0:T(8,128)(2,1)S(1)}, bf16[24,96]{1,0:T(8,128)(2,1)S(1)}) custom-call(bf16[96,3072]{1,0:T(8,128)(2,1)} %bitcast.4, bf16[96,3072]{1,0:T(8,128)(2,1)} %bitcast.5, bf16[96,3072]{1,0:T(8,128)(2,1)} %bitcast.6, bf16[96,3072]{1,0:T(8,128)(2,1)} %bitcast.7, bf16[24,3072]{1,0:T(8,128)(2,1)} %noise_hbm.1, ...), custom_call_target="tpu_custom_call" | custom-call | tf_op jit(solution)/shard_map/pallas_call | solution.py:528
  71.1 1.0 %shard_map.86 = (bf16[4,24,3072]{2,1,0:T(8,128)(2,1)}, bf16[4,24,3072]{2,1,0:T(8,128)(2,1)}, bf16[24,96]{1,0:T(8,128)(2,1)}) custom-call(bf16[4,24,3072]{2,1,0:T(8,128)(2,1)S(1)} %get-tuple-element.6.next_in, bf16[4,24,3072]{2,1,0:T(8,128)(2,1)S(1)} %get-tuple-element.7.den_in, bf16[24,96]{1,0:T(8,128)(2,1)S(1)} %get-tuple-element.8.fin_in), custom_call_target="tpu_custom_call" | custom-call | tf_op jit(solution)/shard_map/pallas_call | solution.py:564
